TPU v7x, 256 devices: a whole 4x4x8 slice. The times are simulated.
256 devices in a mesh: tgt: 64 (over z, y, core), src: 4 (over x).
Axes of the slice: x: 4, y: 4, z: 8, core: 2. Of those that a mesh axis runs over, the one named last changes fastest.
Arguments:
- tgt_coords: bfloat16 [3, 262144], P(None, 'tgt'), may hold values from -1 to 1
- tgt_embed: bfloat16 [64, 262144], P(None, 'tgt'), may hold values from -3 to 3
- tile_perm: int32 [512], P('tgt'), may hold values from 0 to 511, each once
- tile_count: int32 [512], replicated, may hold values from 1 to 512, as said below
- src_coords: bfloat16 [3, 32768], P(None, ('tgt', 'src')), may hold values from -1 to 1
- src_embed: bfloat16 [64, 32768], P(None, ('tgt', 'src')), may hold values from -3 to 3
- anchors: float32 [3, 256], replicated, may hold values from -1 to 1
- sigma2: float32 [1], replicated, may hold values from 0.2 to 1
- outlier_weight: float32 [1], replicated, may hold values from 0.1 to 0.5
- warp_lambda: float32 [1], replicated, may hold values from 0.05 to 0.5
Outputs:
- warped: float32 [3, 32768], P(None, ('tgt', 'src'))
- masses: float32 [32768], P(('tgt', 'src'))
Inputs may be any that keep to these rules, and one draw needn't show every extreme that they name: `tile_count`: one spatial tile has all 512 cells valid.
All inputs are finite; a program needn't handle non-finite values.
Results may differ from a plain program's by a relative error of at most 0.0003.
Values may be sent and summed in bfloat16 or wider, within the bound.
No kernel may reach another device: no remote copies, remote signals or barrier semaphores. Data moves between devices by JAX's collectives and lax.ppermute only.
A program may use at most 64 MiB of HBM per device.

v0:
```python
import functools
import math

import jax
import jax.numpy as jnp
from jax import lax
from jax.experimental import pallas as pl
from jax.experimental.pallas import tpu as pltpu
from jax.sharding import Mesh
from jax.sharding import PartitionSpec as P

TILE = 512
SCORE_GAIN = 4.0
ANCHOR_WIDTH = 0.1
LOG2E = math.log2(math.e)

UNIT = 256
LANES = 128
GROUP = 2048
DEPTH = 256
KEPT = (2, 2, 2, 2, 2, 1)
MASKED = -30000.0
GRAM_ROWS = 6

F32 = jnp.float32
BF16 = jnp.bfloat16
WHOLE = pl.BlockSpec(memory_space=pltpu.VMEM)
SCALAR = pl.BlockSpec(memory_space=pltpu.SMEM)


def split3(value):
    high = value.astype(BF16).astype(F32)
    rest = value - high
    middle = rest.astype(BF16).astype(F32)
    return high, middle, rest - middle


def pick_rows(rows, count):
    width = rows[0].shape[1]
    place = lax.broadcasted_iota(jnp.int32, (count, width), 0)
    out = jnp.zeros((count, width), F32)
    for index, row in enumerate(rows):
        out = jnp.where(place == index, row, out)
    return out


def prepare(
    core_ref, outlier_ref, sigma2_ref, perm_hbm, count_hbm, xyz_hbm, feat_hbm, src_xyz_hbm, src_feat_hbm,
    lots_ref, tgt_ref, units_ref, outlier_out_ref,
    perm_ref, count_ref, xyz_ref, feat_ref, src_xyz_ref, src_feat_ref, arrived,
):
    pairs = [
        (src_xyz_hbm, src_xyz_ref), (src_feat_hbm, src_feat_ref), (perm_hbm, perm_ref),
        (count_hbm, count_ref), (xyz_hbm, xyz_ref), (feat_hbm, feat_ref),
    ]
    copies = [pltpu.make_async_copy(*pair, arrived.at[index]) for index, pair in enumerate(pairs)]
    for copy in copies:
        copy.start()
    for copy in copies:
        copy.wait()
    one = jnp.ones((1, LANES), F32)
    inv = (0.5 * LOG2E) / jnp.full((1, LANES), sigma2_ref[0], F32)
    y = src_xyz_ref[...].astype(F32)
    y = [y[c : c + 1] for c in range(3)]
    square = -(y[0] * y[0] + y[1] * y[1] + y[2] * y[2]) * inv
    side = pick_rows([*y, *y, *y, *split3(square), one, one, one], 16)
    source = jnp.concatenate([src_feat_ref[...], side.astype(BF16)], axis=0)
    for lot in range(lots_ref.shape[0]):
        lots_ref[lot] = source

    gain = SCORE_GAIN / 64 * LOG2E
    inv = (0.5 * LOG2E) / jnp.full((1, TILE), sigma2_ref[0], F32)
    one = jnp.ones((1, TILE), F32)
    lane = lax.broadcasted_iota(jnp.int32, (1, TILE), 1)
    tiles = perm_ref.shape[0]
    offset = jnp.int32(0)
    for tile in range(tiles):
        span = slice(tile * TILE, (tile + 1) * TILE)
        count = count_ref[perm_ref[tile]]
        xyz = xyz_ref[:, span].astype(F32)
        x = [xyz[c : c + 1] for c in range(3)]
        square = -(x[0] * x[0] + x[1] * x[1] + x[2] * x[2]) * inv
        parts = [split3(row * (2.0 * inv)) for row in x]
        own = split3(jnp.where(lane < count, square, MASKED))
        rows = [part[level] for level in range(3) for part in parts] + [one, one, one, *own]
        rows = rows + [jnp.zeros_like(one)] + [*x, one] * 2
        high, middle, low = split3(feat_ref[:, span].astype(F32) * gain)
        wide = jnp.concatenate(
            [high, pick_rows(rows, 24), jnp.zeros((40, TILE), F32), middle, low], axis=0
        )
        tgt_ref[pl.ds(pl.multiple_of(offset, 16), TILE), :] = wide.T.astype(BF16)
        offset = offset + ((count + 15) // 16) * 16
    blank = jnp.where(lax.broadcasted_iota(jnp.int32, (UNIT, DEPTH), 1) == 76, MASKED, 0.0)
    tgt_ref[pl.ds(pl.multiple_of(offset, 16), UNIT), :] = blank.astype(BF16)
    units_ref[0] = (offset + UNIT - 1) // UNIT
    units_ref[1] = core_ref[0]
    outlier_out_ref[0] = outlier_ref[0]


def widened(wide_ref, group, start):
    at = slice(start, start + 256)
    feat = wide_ref[group, 0:64, at]
    return jnp.concatenate([wide_ref[group, :, at], feat, feat], axis=0)


def kernel_pass(units_ref, tgt_ref, own_ref, other_ref, *refs):
    *kernel_refs, sum_ref, wide_ref, total_ref = refs
    groups = wide_ref.shape[0]
    wide_ref[:, 80:128, :] = jnp.zeros((groups, 48, GROUP), BF16)
    for lot, panel_ref in enumerate((own_ref, other_ref)):
        for piece in range(panel_ref.shape[0]):
            group, start = divmod((lot * panel_ref.shape[0] + piece) * LANES, GROUP)
            wide_ref[group, 0:80, start : start + LANES] = panel_ref[piece]

    def block(unit, count, kernel_ref=None, row=0):
        height = count * UNIT
        total_ref[0:height, :] = jnp.zeros((height, LANES), F32)

        def columns(group, unused):
            tgt = tgt_ref[unit_rows(unit, count), :]
            total = jnp.zeros((height, LANES), F32)
            for start in range(0, GROUP, 256):
                score = jnp.dot(tgt, widened(wide_ref, group, start), preferred_element_type=F32)
                rounded = jnp.exp2(score).astype(BF16)
                if kernel_ref is not None:
                    kernel_ref[group, row : row + height, start : start + 256] = rounded
                value = rounded.astype(F32)
                total += value[:, 0:128] + value[:, 128:256]
            total_ref[0:height, :] += total
            return unused

        lax.fori_loop(0, groups, columns, 0)
        for part in range(count):
            lines = total_ref[part * UNIT : (part + 1) * UNIT, :]
            sum_ref[pl.ds(unit + part, 1), :] = jnp.sum(lines.T, axis=0, keepdims=True)

    each_unit(units_ref[0], kernel_refs, block)


def unit_rows(unit, count):
    start = unit * UNIT
    return pl.ds(start if isinstance(unit, int) else pl.multiple_of(start, UNIT), count * UNIT)


def each_unit(units, kernel_refs, block):
    for index, kernel_ref in enumerate(kernel_refs):
        first = sum(KEPT[:index])
        if KEPT[index] == 2:
            pl.when(units >= first + 2)(functools.partial(block, first, 2, kernel_ref))
        pl.when(units == first + 1)(functools.partial(block, first, 1, kernel_ref))
    if KEPT[-1] == 1:
        pl.when(units > sum(KEPT))(functools.partial(block, sum(KEPT) - 1, 1, kernel_refs[-1]))

    def beyond(unit, unused):
        block(unit, 1)
        return unused

    lax.fori_loop(sum(KEPT), units, beyond, 0)


def warp_sums(acc_ref, wide_ref, anchors_ref, core, out_ref, gram_ref):
    pieces = out_ref.shape[1] // 8
    groups = wide_ref.shape[0]
    count = anchors_ref.shape[1]
    rate = 0.5 / ANCHOR_WIDTH * LOG2E
    a0, a1, a2 = anchors_ref[0:1, :], anchors_ref[1:2, :], anchors_ref[2:3, :]
    square = -(a0 * a0 + a1 * a1 + a2 * a2) * rate
    parts = [split3(row * (2.0 * rate)) for row in (a0, a1, a2)]
    zero = jnp.zeros((1, count), F32)
    rows = [part[level] for level in range(3) for part in parts] + [zero] * 3 + [*split3(square)]
    anchor_side = pick_rows(rows, LANES).T.astype(BF16)[:, 0:16]
    sums = acc_ref[...]
    sums = sums + pltpu.roll(sums, 4, 0)
    acc_ref[...] = sums
    gram_ref[...] = jnp.zeros_like(gram_ref)
    width = GROUP // 2

    def chunk(index, unused):
        at = pl.ds(pl.multiple_of(index * width, width), width)
        half = pl.ds(pl.multiple_of(index % 2 * width, width), width)
        side = wide_ref[index // 2, 64:80, half]
        y = side.astype(F32)[0:8]
        y0, y1, y2 = y[0:1], y[1:2], y[2:3]
        square = (y0 * y0 + y1 * y1 + y2 * y2) * rate
        basis = jnp.exp2(jnp.dot(anchor_side, side, preferred_element_type=F32) - square)
        moment = acc_ref[:, at]
        mass = moment[3:4, :]
        pull = moment - mass * y
        root = jnp.sqrt(mass)
        pull = pull * lax.rsqrt(jnp.maximum(mass, 1e-36))
        scaled = basis * root
        scaled_high, scaled_low = halves(scaled)
        pull_high, pull_low = halves(jnp.concatenate([pull, jnp.zeros_like(pull)], axis=0))
        last = (((1,), (1,)), ((), ()))
        left = jnp.concatenate([scaled_high, pull_high, pull_low], axis=0)
        first = lax.dot_general(left, scaled_high, last, preferred_element_type=F32)
        second = lax.dot_general(left[0:272], scaled_low, last, preferred_element_type=F32)
        gram_ref[0:288, :] += first
        gram_ref[288:560, :] += second
        return unused

    lax.fori_loop(0, groups * 2, chunk, 0)
    cross = gram_ref[288:544, :]
    gram_ref[0:256, :] += cross + cross.T
    total = jnp.sum(acc_ref[3:4, :])
    row = lax.broadcasted_iota(jnp.int32, (8, LANES), 0)
    for half in range(2):
        at = jnp.where(core == half, 0, 1)
        for r in range(GRAM_ROWS):
            out_ref[at, pl.ds(r, pieces, stride=8), :] = gram_ref[gram_place(half, r, pieces)]
        out_ref[at, pl.ds(GRAM_ROWS, pieces, stride=8), :] = jnp.zeros((pieces, LANES), F32)
        lanes = slice(half * LANES, (half + 1) * LANES)
        pulled = gram_ref[256:264, lanes] + gram_ref[272:280, lanes] + gram_ref[544:552, lanes]
        pulled = jnp.where(row == 3, total, pulled)
        for r in range(4):
            out_ref[at, r * 8 + GRAM_ROWS : r * 8 + GRAM_ROWS + 1, :] = pulled[r : r + 1]
        for piece in range(pieces):
            s = (half * pieces + piece) * LANES
            out_ref[half, piece * 8 + 7 : piece * 8 + 8, :] = acc_ref[3:4, s : s + LANES]


def gram_place(half, r, pieces):
    if half == 0:
        first, right = (r * pieces, 0) if r < 4 else ((r - 4) * pieces, 1)
    else:
        first, right = 64 + r * pieces, 1
    return slice(first, first + pieces), slice(right * LANES, (right + 1) * LANES)


def moment_pass(
    units_ref, outlier_ref, sum0_ref, sum1_ref, sum2_ref, sum3_ref, tgt_ref, wide_ref, anchors_ref,
    *refs, total_sources,
):
    *kernel_refs, out_ref, acc_ref, gram_ref, part_ref = refs
    groups = wide_ref.shape[0]
    outlier = jnp.full((1, UNIT), outlier_ref[0], F32)
    floor = outlier / (1.0 - outlier) * total_sources
    acc_ref[...] = jnp.zeros_like(acc_ref)

    def block(unit, count, kernel_ref=None):
        normals = []
        for part in range(count):
            normal = floor
            for ref in (sum0_ref, sum1_ref, sum2_ref, sum3_ref):
                normal = normal + ref[pl.ds(unit + part, 1), :]
            normals.append(normal)
        side = tgt_ref[unit_rows(unit, count), 0:128].astype(F32).T[80:88]
        weight = side / jnp.concatenate(normals, axis=1)
        high = weight.astype(BF16).astype(F32)
        row = lax.broadcasted_iota(jnp.int32, weight.shape, 0)
        weight = jnp.where(row < 4, high, weight - high).astype(BF16)
        for group in range(groups):
            if kernel_ref is None:
                for start in range(0, GROUP, 256):
                    tgt = tgt_ref[unit_rows(unit, count), :]
                    score = jnp.dot(tgt, widened(wide_ref, group, start), preferred_element_type=F32)
                    part_ref[:, start : start + 256] = jnp.exp2(score).astype(BF16)
            for start in range(0, GROUP, 1024):
                at = slice(group * GROUP + start, group * GROUP + start + 1024)
                if kernel_ref is None:
                    value = part_ref[:, start : start + 1024]
                else:
                    value = kernel_ref[group, 0 : count * UNIT, start : start + 1024]
                acc_ref[:, at] += jnp.dot(weight, value, preferred_element_type=F32)

    each_unit(units_ref[0], kernel_refs, block)
    warp_sums(acc_ref, wide_ref, anchors_ref, units_ref[1], out_ref, gram_ref)


def squared_gap(first, second):
    gap_a, gap_b, gap_c = (first[c] - second[c] for c in range(3))
    return gap_a * gap_a + gap_b * gap_b + gap_c * gap_c


def halves(value):
    high = value.astype(BF16)
    return high, (value - high.astype(F32)).astype(BF16)


def dot3(first, second):
    (a, b), (c, d) = first, second
    wide = functools.partial(jnp.dot, preferred_element_type=F32)
    return wide(a, c) + (wide(a, d) + wide(b, c))


def dot_full(first, second):
    return jnp.dot(first, second, precision=lax.Precision.HIGHEST, preferred_element_type=F32)


def warp_update(
    sigma2_ref, lambda_ref, anchors_ref, xyz_ref, mass_ref, sums_ref, out_ref, out_mass_ref,
    system_ref, inverse_ref,
):
    pieces = sums_ref.shape[1] // 8
    count = anchors_ref.shape[1]
    for half in range(2):
        for r in range(GRAM_ROWS):
            system_ref[gram_place(half, r, pieces)] = sums_ref[half, pl.ds(r, pieces, stride=8), :]
    system_ref[128:256, 0:128] = system_ref[0:128, 128:256].T
    pulled = [
        jnp.concatenate([sums_ref[half, r * 8 + GRAM_ROWS : r * 8 + GRAM_ROWS + 1, :] for half in range(2)], axis=1)
        for r in range(3)
    ]
    total = sums_ref[0, 24 + GRAM_ROWS : 25 + GRAM_ROWS, 0:1]
    pulled = pick_rows(pulled, 8) / total

    rows = [anchors_ref[c : c + 1, :] for c in range(3)]
    columns = jnp.concatenate([pick_rows(rows, 8), jnp.zeros((120, count), F32)], axis=0).T
    columns = [columns[:, c : c + 1] for c in range(3)]
    rate = 0.5 / ANCHOR_WIDTH
    anchor_gram = jnp.exp(-squared_gap(columns, rows) * rate)
    place = lax.broadcasted_iota(jnp.int32, (count, count), 0)
    eye = jnp.where(place == lax.broadcasted_iota(jnp.int32, (count, count), 1), 1.0, 0.0)
    weight = lambda_ref[0] * sigma2_ref[0]
    system = system_ref[...] / total + weight * (anchor_gram + eye)
    system_ref[...] = system

    low = weight
    high = jnp.max(jnp.sum(jnp.abs(system), axis=0, keepdims=True)) * 1.0001
    start = 2.0 / jnp.full((1, count), low + high, F32)
    bound = jnp.max(jnp.full((8, LANES), high - low, F32) / jnp.full((8, LANES), high + low, F32))

    def narrowed(bound):
        square = jnp.full((8, LANES), bound * bound, F32)
        return jnp.max(2.0 / (2.0 - square)), jnp.max(square / (2.0 - square))

    scale, bound = narrowed(bound)
    inverse_ref[...] = (scale * start) * (2.0 * eye - start * system)
    system_halves = halves(system)

    def improve(bound):
        scale, after = narrowed(bound)
        inverse = inverse_ref[...]
        parts = halves(inverse)
        residual = 2.0 * eye - dot3(system_halves, parts)
        inverse_ref[...] = scale * dot3(parts, halves(residual))
        return after

    lax.while_loop(lambda bound: bound > 1e-2, improve, bound)
    inverse = inverse_ref[...]
    coeffs = dot_full(pulled, inverse)
    for _ in range(3):
        coeffs = coeffs + dot_full(pulled - dot_full(coeffs, system), inverse)

    xyz = xyz_ref[...].astype(F32)
    basis = jnp.exp(-squared_gap(columns, [xyz[c : c + 1] for c in range(3)]) * rate)
    out_ref[...] = xyz + dot_full(coeffs, basis)[0:3]
    out_mass_ref[...] = mass_ref[7:8, :]


def spread(value, axes):
    lots = jnp.broadcast_to(value, (lax.axis_size(axes), *value.shape[1:]))
    return lax.all_to_all(lots, axes, 0, 0, tiled=True)


def turned(value, axis, by):
    size = lax.axis_size(axis)
    return lax.ppermute(value, axis, [(i, (i + by) % size) for i in range(size)])


def local(
    tgt_coords, tgt_embed, tile_perm, tile_count, src_coords, src_embed, anchors, sigma2,
    outlier_weight, warp_lambda,
):
    cells = tgt_coords.shape[1]
    zs, ys, cs, xs = (lax.axis_size(name) for name in ("z", "y", "c", "x"))
    pieces = zs * ys
    sources = pieces * cs * LANES
    groups = sources // GROUP

    core = lax.axis_index("c").astype(jnp.int32)[None]
    inputs = (tile_perm, tile_count, tgt_coords, tgt_embed, src_coords, src_embed)
    inputs = [pltpu.with_memory_space_constraint(value, pltpu.HBM) for value in inputs]
    lots, targets, units, outlier = pl.pallas_call(
        prepare,
        in_specs=[SCALAR] * 3 + [pl.BlockSpec(memory_space=pltpu.HBM)] * len(inputs),
        out_specs=[WHOLE, WHOLE, SCALAR, SCALAR],
        out_shape=[
            jax.ShapeDtypeStruct((pieces, 80, LANES), BF16),
            jax.ShapeDtypeStruct((cells + TILE, DEPTH), BF16),
            jax.ShapeDtypeStruct((2,), jnp.int32),
            jax.ShapeDtypeStruct((1,), F32),
        ],
        scratch_shapes=[
            *[pltpu.SMEM(value.shape, value.dtype) for value in inputs[:2]],
            *[pltpu.VMEM(value.shape, value.dtype) for value in inputs[2:]],
            pltpu.SemaphoreType.DMA((len(inputs),)),
        ],
        compiler_params=pltpu.CompilerParams(vmem_limit_bytes=8 << 20),
        name="prepare",
    )(core, outlier_weight, sigma2, *inputs)

    own = lax.all_to_all(lots, ("z", "y"), 0, 0, tiled=True)
    other = lax.ppermute(own, "c", [(0, 1), (1, 0)])

    *kernels, sums, wide = pl.pallas_call(
        kernel_pass,
        in_specs=[SCALAR, WHOLE, WHOLE, WHOLE],
        out_specs=[WHOLE] * (len(KEPT) + 2),
        out_shape=[
            *[jax.ShapeDtypeStruct((groups, count * UNIT, GROUP), BF16) for count in KEPT],
            jax.ShapeDtypeStruct((cells // UNIT, UNIT), F32),
            jax.ShapeDtypeStruct((groups, DEPTH // 2, GROUP), BF16),
        ],
        scratch_shapes=[pltpu.VMEM((2 * UNIT, LANES), F32)],
        compiler_params=pltpu.CompilerParams(vmem_limit_bytes=2 << 20),
        name="kernel_pass",
    )(units, targets, own, other)

    all_sums = [sums] + [turned(sums, "x", by) for by in range(1, xs)]

    share = pl.pallas_call(
        functools.partial(moment_pass, total_sources=sources * xs),
        in_specs=[SCALAR, SCALAR, *[WHOLE] * (xs + 3 + len(KEPT))],
        out_specs=WHOLE,
        out_shape=jax.ShapeDtypeStruct((cs, pieces * 8, LANES), F32),
        scratch_shapes=[
            pltpu.VMEM((8, sources), F32),
            pltpu.VMEM((560, 256), F32),
            pltpu.VMEM((UNIT, GROUP), BF16),
        ],
        compiler_params=pltpu.CompilerParams(vmem_limit_bytes=5 << 20),
        name="moment_pass",
    )(units, outlier, *all_sums, targets, wide, anchors, *kernels)

    part = share[0] + lax.ppermute(share[1], "c", [(0, 1), (1, 0)])
    part = part.reshape(pieces, 8, LANES)
    part = jnp.sum(lax.all_to_all(part, ("z", "y"), 0, 0, tiled=True), axis=0)
    total = part + turned(part, "x", 1) + turned(part, "x", 2) + turned(part, "x", 3)
    both = lax.all_gather(spread(total[None], ("z", "y")).reshape(pieces * 8, LANES), "c")

    warped, masses = pl.pallas_call(
        warp_update,
        in_specs=[SCALAR, SCALAR, WHOLE, WHOLE, WHOLE, WHOLE],
        out_specs=[WHOLE, WHOLE],
        out_shape=[jax.ShapeDtypeStruct((3, LANES), F32), jax.ShapeDtypeStruct((1, LANES), F32)],
        scratch_shapes=[pltpu.VMEM((256, 256), F32)] * 2,
        compiler_params=pltpu.CompilerParams(vmem_limit_bytes=6 << 20),
        name="warp_update",
    )(sigma2, warp_lambda, anchors, src_coords, part, both)
    return (warped, masses.reshape(LANES))


def solution(mesh):
    fine = Mesh(mesh.devices.reshape(8, 4, 2, 4), ("z", "y", "c", "x"))
    tgt = ("z", "y", "c")
    both = ("z", "y", "c", "x")
    placed = (
        P(None, tgt), P(None, tgt), P(tgt), P(), P(None, both), P(None, both), P(), P(), P(), P(),
    )
    return jax.shard_map(
        local, mesh=fine, in_specs=placed, out_specs=(P(None, both), P(both)), check_vma=False
    )
```

profile of v0, /device:TPU:1, one launch (start us, length us, event | category | flops | bytes accessed | tf_op | source)
XLA Modules:
  0.0 135.6 jit_solution(10029720152863187770)
XLA Ops:
  1.9 2.7 %prepare.1 = (bf16[32,80,128]{2,1,0:T(8,128)(2,1)S(1)}, bf16[4608,256]{1,0:T(8,128)(2,1)S(1)}, s32[2]{0:T(128)S(1)}, f32[1]{0:T(128)}) custom-call(s32[1]{0:T(128)} %bitcast.core_ref, f32[1]{0:T(128)S(6)} %copy.13.outlier_ref, f32[1]{0:T(128)S(6)} %copy.12.sigma2_ref, s32[8]{0:T(128)} %perm_hbm.1, s32[512]{0:T(512)} %count_hbm.1, bf16[3,4096]{1,0:T(4,128)(2,1)} %xyz_hbm.1, ...), custom_call_target="tpu_custom_call" | custom-call | tf_op jit(solution)/shard_map/prepare/pallas_call | solution.py:374
  4.7 30.5 %all_to_all.15.own_ref = bf16[32,80,128]{2,1,0:T(8,128)(2,1)S(1)} all-to-all(bf16[32,80,128]{2,1,0:T(8,128)(2,1)S(1)} %get-tuple-element.19), channel_id=1, replica_groups=mesh['z'=8,'y'=4,'c'=2,'x'=4] {'z','y'}, dimensions={0} | all-to-all | bytes 1310720 | tf_op jit(solution)/shard_map/all_to_all | solution.py:393
  35.2 2.5 %collective-permute-start = (bf16[32,80,128]{2,1,0:T(8,128)(2,1)S(1)}, bf16[32,80,128]{2,1,0:T(8,128)(2,1)S(1)}, u32[]{:S(2)}, u32[]{:S(2)}) collective-permute-start(bf16[32,80,128]{2,1,0:T(8,128)(2,1)S(1)} %all_to_all.15.own_ref), channel_id=1, source_target_pairs={{0,4},{4,0},{1,5},{5,1},{2,6},{6,2},{3,7},{7,3},{8,12},{12,8},{9,1... | collective-permute-start | bytes 1966088 | tf_op jit(solution)/shard_map/ppermute | solution.py:394
  37.7 1.7 %collective-permute-done.other_ref = bf16[32,80,128]{2,1,0:T(8,128)(2,1)S(1)} collective-permute-done((bf16[32,80,128]{2,1,0:T(8,128)(2,1)S(1)}, bf16[32,80,128]{2,1,0:T(8,128)(2,1)S(1)}, u32[]{:S(2)}, u32[]{:S(2)}) %collective-permute-start) | collective-permute-done | bytes 655392 | tf_op jit(solution)/shard_map/ppermute | solution.py:394
  39.4 19.1 %kernel_pass.1 = (bf16[4,512,2048]{2,1,0:T(8,128)(2,1)S(1)}, bf16[4,512,2048]{2,1,0:T(8,128)(2,1)S(1)}, bf16[4,512,2048]{2,1,0:T(8,128)(2,1)S(1)}, bf16[4,512,20...) custom-call(s32[2]{0:T(128)S(1)} %get-tuple-element.16.units_ref, ...), custom_call_target="tpu_custom_call" | custom-call | tf_op jit(solution)/shard_map/kernel_pass/pallas_call | solution.py:396
  58.5 1.5 %collective-permute-start.1 = (f32[16,256]{1,0:T(8,128)S(1)}, f32[16,256]{1,0:T(8,128)S(1)}, u32[]{:S(2)}, u32[]{:S(2)}) collective-permute-start(f32[16,256]{1,0:T(8,128)S(1)} %get-tuple-element.20.sum0_ref), channel_id=1, source_target_pairs={{0,1},{1,2},{2,3},{3,0},{4,5},{5,6},{6,7},{7,4},{8,9},{9,10},{10,1... | collective-permute-start | bytes 49160 | tf_op jit(solution)/shard_map/ppermute | solution.py:358
  60.0 2.4 %collective-permute-start.2 = (f32[16,256]{1,0:T(8,128)S(1)}, f32[16,256]{1,0:T(8,128)S(1)}, u32[]{:S(2)}, u32[]{:S(2)}) collective-permute-start(f32[16,256]{1,0:T(8,128)S(1)} %get-tuple-element.20.sum0_ref), channel_id=1, source_target_pairs={{0,2},{1,3},{2,0},{3,1},{4,6},{5,7},{6,4},{7,5},{8,10},{9,11},{10,... | collective-permute-start | bytes 49160 | tf_op jit(solution)/shard_map/ppermute | solution.py:358
  62.4 1.2 collective-permute-start.3
  63.6 0.0 collective-permute-done.1.sum1_ref
  63.6 0.6 collective-permute-done.2.sum2_ref
  64.1 1.3 collective-permute-done.3.sum3_ref
  65.4 0.0 copy-start
  65.4 0.7 copy-done
  66.1 0.0 copy-start.1
  66.1 0.0 copy-start.2
  66.1 13.4 %moment_pass.1 = f32[2,256,128]{2,1,0:T(8,128)S(1)} custom-call(s32[2]{0:T(128)S(1)} %get-tuple-element.16.units_ref, f32[1]{0:T(128)} %get-tuple-element.17.outlier_ref, f32[16,256]{1,0:T(8,128)S(1)} %get-tuple-element.20.sum0_ref, f32[16,256]{1,0:T(8,128)S(1)} %collective-permute-done.1.sum1_ref, f32[16,256]{1,0:T(8,128)S(1)} %collective-permute-done.2.sum2_ref, ...), custom_call_target="tpu_custom_call" | custom-call | tf_op jit(solution)/shard_map/moment_pass/pallas_call | solution.py:412
  79.6 0.1 collective-permute-start.4
  79.7 1.3 collective-permute-done.4
  81.0 23.0 %all_to_all.16 = f32[32,8,128]{2,1,0:T(8,128)S(1)} all-to-all(f32[32,8,128]{2,1,0:T(8,128)S(1)} %fusion.1), channel_id=1, replica_groups=mesh['z'=8,'y'=4,'c'=2,'x'=4] {'z','y'}, dimensions={0} | all-to-all | bytes 262144 | tf_op jit(solution)/shard_map/all_to_all | solution.py:428
  104.1 0.4 collective-permute-start.5
  104.4 3.3 %collective-permute-start.6 = (f32[8,128]{1,0:T(8,128)S(1)}, f32[8,128]{1,0:T(8,128)S(1)}, u32[]{:S(2)}, u32[]{:S(2)}) collective-permute-start(f32[8,128]{1,0:T(8,128)S(1)} %reduce_sum.9.mass_ref), channel_id=1, source_target_pairs={{0,2},{1,3},{2,0},{3,1},{4,6},{5,7},{6,4},{7,5},{8,10},{9,11},{10,... | collective-permute-start | bytes 12296 | tf_op jit(solution)/shard_map/ppermute | solution.py:358
  107.7 0.0 collective-permute-start.7
  107.7 0.1 collective-permute-done.5
  107.8 0.9 collective-permute-done.6
  108.7 1.7 %collective-permute-done.7 = f32[8,128]{1,0:T(8,128)S(1)} collective-permute-done((f32[8,128]{1,0:T(8,128)S(1)}, f32[8,128]{1,0:T(8,128)S(1)}, u32[]{:S(2)}, u32[]{:S(2)}) %collective-permute-start.7) | collective-permute-done | bytes 4128 | tf_op jit(solution)/shard_map/ppermute | solution.py:358
  110.5 0.7 broadcast_in_dim.10
  111.1 3.8 %all-to-all-start.2 = ((f32[32,8,128]{2,1,0:T(8,128)}), f32[32,8,128]{2,1,0:T(8,128)S(1)}, u32[]{:S(2)}, u32[]{:S(2)}) async-start(f32[32,8,128]{2,1,0:T(8,128)} %broadcast_in_dim.10), calls=%async_computation.2 | async-start | bytes 262144 | tf_op jit(solution)/shard_map/all_to_all | solution.py:353
  115.6 8.8 %all-to-all-done.2 = f32[32,8,128]{2,1,0:T(8,128)S(1)} async-done(((f32[32,8,128]{2,1,0:T(8,128)}), f32[32,8,128]{2,1,0:T(8,128)S(1)}, u32[]{:S(2)}, u32[]{:S(2)}) %all-to-all-start.2) | async-done | bytes 131104 | tf_op jit(solution)/shard_map/all_to_all | solution.py:353
  124.4 5.8 %all_gather.3.sums_ref = f32[2,256,128]{2,1,0:T(8,128)S(1)} all-gather(f32[1,256,128]{2,1,0:T(8,128)S(1)} %bitcast.13), channel_id=1, replica_groups=mesh['z'=8,'y'=4,'c'=2,'x'=4] {'c'}, dimensions={0}, use_global_device_ids=true | all-gather | bytes 393216 | tf_op jit(solution)/shard_map/all_gather | solution.py:430
  130.2 0.0 copy-done.1
  130.2 0.0 copy-done.2
  130.2 5.5 %warp_update.1 = (f32[3,128]{1,0:T(4,128)}, f32[1,128]{1,0:T(1,128)}) custom-call(f32[1]{0:T(128)S(6)} %copy.12.sigma2_ref, f32[1]{0:T(128)S(6)} %copy.14.lambda_ref, f32[3,256]{1,0:T(4,128)S(1)} %copy-done.1, bf16[3,128]{1,0:T(4,128)(2,1)S(1)} %copy-done.2, f32[8,128]{1,0:T(8,128)S(1)} %reduce_sum.9.mass_ref, f32[2,256,128]{2,1,0:T(8,128)S(1)} %all_gather.3.sums_ref), custom_call_target="tpu_custom_call" | custom-call | tf_op jit(solution)/shard_map/warp_update/pallas_call | solution.py:432
  (4 shorter events, 0.1 us)
Async XLA Ops:
  35.2 4.2 %collective-permute-start = (bf16[32,80,128]{2,1,0:T(8,128)(2,1)S(1)}, bf16[32,80,128]{2,1,0:T(8,128)(2,1)S(1)}, u32[]{:S(2)}, u32[]{:S(2)}) collective-permute-start(bf16[32,80,128]{2,1,0:T(8,128)(2,1)S(1)} %all_to_all.15.own_ref), channel_id=1, source_target_pairs={{0,4},{4,0},{1,5},{5,1},{2,6},{6,2},{3,7},{7,3},{8,12},{12,8},{9,1... | collective-permute-start | bytes 1966088 | tf_op jit(solution)/shard_map/ppermute | solution.py:394
  58.5 5.1 %collective-permute-start.1 = (f32[16,256]{1,0:T(8,128)S(1)}, f32[16,256]{1,0:T(8,128)S(1)}, u32[]{:S(2)}, u32[]{:S(2)}) collective-permute-start(f32[16,256]{1,0:T(8,128)S(1)} %get-tuple-element.20.sum0_ref), channel_id=1, source_target_pairs={{0,1},{1,2},{2,3},{3,0},{4,5},{5,6},{6,7},{7,4},{8,9},{9,10},{10,1... | collective-permute-start | bytes 49160 | tf_op jit(solution)/shard_map/ppermute | solution.py:358
  60.0 4.2 %collective-permute-start.2 = (f32[16,256]{1,0:T(8,128)S(1)}, f32[16,256]{1,0:T(8,128)S(1)}, u32[]{:S(2)}, u32[]{:S(2)}) collective-permute-start(f32[16,256]{1,0:T(8,128)S(1)} %get-tuple-element.20.sum0_ref), channel_id=1, source_target_pairs={{0,2},{1,3},{2,0},{3,1},{4,6},{5,7},{6,4},{7,5},{8,10},{9,11},{10,... | collective-permute-start | bytes 49160 | tf_op jit(solution)/shard_map/ppermute | solution.py:358
  62.4 3.0 %collective-permute-start.3 = (f32[16,256]{1,0:T(8,128)S(1)}, f32[16,256]{1,0:T(8,128)S(1)}, u32[]{:S(2)}, u32[]{:S(2)}) collective-permute-start(f32[16,256]{1,0:T(8,128)S(1)} %get-tuple-element.20.sum0_ref), channel_id=1, source_target_pairs={{0,3},{1,0},{2,1},{3,2},{4,7},{5,4},{6,5},{7,6},{8,11},{9,8},{10,9... | collective-permute-start | bytes 49160 | tf_op jit(solution)/shard_map/ppermute | solution.py:358
  65.4 0.7 copy-start
  66.1 64.1 %copy-start.1 = (f32[3,256]{1,0:T(4,128)S(1)}, f32[3,256]{1,0:T(4,128)}, u32[]{:S(2)}) copy-start(f32[3,256]{1,0:T(4,128)} %anchors_ref.3) | copy-start | bytes 9220
  66.1 64.1 %copy-start.2 = (bf16[3,128]{1,0:T(4,128)(2,1)S(1)}, bf16[3,128]{1,0:T(4,128)(2,1)}, u32[]{:S(2)}) copy-start(bf16[3,128]{1,0:T(4,128)(2,1)} %xyz_ref.1) | copy-start | bytes 2308
  79.6 1.4 %collective-permute-start.4 = (f32[256,128]{1,0:T(8,128)S(1)}, f32[256,128]{1,0:T(8,128)S(1)}, u32[]{:S(2)}, u32[]{:S(2)}) collective-permute-start(f32[256,128]{1,0:T(8,128)S(1)} %slice_bitcast_fusion), channel_id=1, source_target_pairs={{0,4},{4,0},{1,5},{5,1},{2,6},{6,2},{3,7},{7,3},{8,12},{12,8},{9,1... | collective-permute-start | bytes 393224 | tf_op jit(solution)/shard_map/ppermute | solution.py:426
  104.1 3.7 %collective-permute-start.5 = (f32[8,128]{1,0:T(8,128)S(1)}, f32[8,128]{1,0:T(8,128)S(1)}, u32[]{:S(2)}, u32[]{:S(2)}) collective-permute-start(f32[8,128]{1,0:T(8,128)S(1)} %reduce_sum.9.mass_ref), channel_id=1, source_target_pairs={{0,1},{1,2},{2,3},{3,0},{4,5},{5,6},{6,7},{7,4},{8,9},{9,10},{10,1... | collective-permute-start | bytes 12296 | tf_op jit(solution)/shard_map/ppermute | solution.py:358
  104.4 4.3 %collective-permute-start.6 = (f32[8,128]{1,0:T(8,128)S(1)}, f32[8,128]{1,0:T(8,128)S(1)}, u32[]{:S(2)}, u32[]{:S(2)}) collective-permute-start(f32[8,128]{1,0:T(8,128)S(1)} %reduce_sum.9.mass_ref), channel_id=1, source_target_pairs={{0,2},{1,3},{2,0},{3,1},{4,6},{5,7},{6,4},{7,5},{8,10},{9,11},{10,... | collective-permute-start | bytes 12296 | tf_op jit(solution)/shard_map/ppermute | solution.py:358
  107.7 2.8 %collective-permute-start.7 = (f32[8,128]{1,0:T(8,128)S(1)}, f32[8,128]{1,0:T(8,128)S(1)}, u32[]{:S(2)}, u32[]{:S(2)}) collective-permute-start(f32[8,128]{1,0:T(8,128)S(1)} %reduce_sum.9.mass_ref), channel_id=1, source_target_pairs={{0,3},{1,0},{2,1},{3,2},{4,7},{5,4},{6,5},{7,6},{8,11},{9,8},{10,9... | collective-permute-start | bytes 12296 | tf_op jit(solution)/shard_map/ppermute | solution.py:358
  111.1 13.3 %all-to-all-start.2 = ((f32[32,8,128]{2,1,0:T(8,128)}), f32[32,8,128]{2,1,0:T(8,128)S(1)}, u32[]{:S(2)}, u32[]{:S(2)}) async-start(f32[32,8,128]{2,1,0:T(8,128)} %broadcast_in_dim.10), calls=%async_computation.2 | async-start | bytes 262144 | tf_op jit(solution)/shard_map/all_to_all | solution.py:353
where the time goes:
time: 136 us
  blocking collectives  59.3 us (44%)
  Pallas kernels  40.7 us (30%)
  waiting for transfers between devices  16.4 us (12%)
  starting transfers between devices  15.1 us (11%)
  between operations  2.64 us (2%)
  local copies, waits for them, and re-layouts  1.37 us (1%)
    all_to_all x1, blocking collectives, local(): own = lax.all_to_all(lots, ('z', 'y'), 0, 0, tiled=True)  30.5 us
    all_to_all x1, blocking collectives, local(): part = jnp.sum(lax.all_to_all(part, ('z', 'y'), 0, 0, tiled=True), axis=0)  23 us
    pallas_call x1, Pallas kernels, local(): pl.pallas_call(kernel_pass, in_specs=[SCALAR, WHOLE, WHOLE, WHOLE], out_s...  19.1 us
    pallas_call x1, Pallas kernels, local(): pl.pallas_call(functools.partial(moment_pass, total_sources=sources * xs)...  13.4 us
    all_to_all x1, waiting for transfers between devices, spread(): return lax.all_to_all(lots, axes, 0, 0, tiled=True)  8.76 us
    ppermute x6, starting transfers between devices, turned(): lax.ppermute(value, axis, [(i, (i + by) % size) for i in range(size)])  8.73 us
    all_gather x1, blocking collectives, local(): lax.all_gather(spread(total[None], ('z', 'y')).reshape(pieces * 8, LANES)...  5.8 us
    pallas_call x1, Pallas kernels, local(): pl.pallas_call(warp_update, in_specs=[SCALAR, SCALAR, WHOLE, WHOLE, WHOLE...  5.46 us
  transfers between devices with their start and end apart: 9, of which 8 were waited for; matrix products, arithmetic and copies ran while one was open for 0% of the time, Pallas kernels for 0%

commit v1 on v0

--- a/solution.py
+++ b/solution.py
@@ -56,7 +56,7 @@
     copies = [pltpu.make_async_copy(*pair, arrived.at[index]) for index, pair in enumerate(pairs)]
     for copy in copies:
         copy.start()
-    for copy in copies:
+    for copy in copies[:2]:
         copy.wait()
     one = jnp.ones((1, LANES), F32)
     inv = (0.5 * LOG2E) / jnp.full((1, LANES), sigma2_ref[0], F32)
@@ -68,6 +68,8 @@
     for lot in range(lots_ref.shape[0]):
         lots_ref[lot] = source
 
+    for copy in copies[2:]:
+        copy.wait()
     gain = SCORE_GAIN / 64 * LOG2E
     inv = (0.5 * LOG2E) / jnp.full((1, TILE), sigma2_ref[0], F32)
     one = jnp.ones((1, TILE), F32)
@@ -124,9 +126,18 @@
                 rounded = jnp.exp2(score).astype(BF16)
                 if kernel_ref is not None:
                     kernel_ref[group, row : row + height, start : start + 256] = rounded
-                value = rounded.astype(F32)
-                total += value[:, 0:128] + value[:, 128:256]
-            total_ref[0:height, :] += total
+                if kernel_ref is None:
+                    value = rounded.astype(F32)
+                    total += value[:, 0:128] + value[:, 128:256]
+            if kernel_ref is not None:
+                for part in range(0, height, 16):
+                    lines = kernel_ref[group, row + part : row + part + 16, :].astype(F32)
+                    line = lines[:, 0:128]
+                    for start in range(128, GROUP, 128):
+                        line += lines[:, start : start + 128]
+                    total_ref[part : part + 16, :] += line
+            else:
+                total_ref[0:height, :] += total
             return unused
 
         lax.fori_loop(0, groups, columns, 0)
@@ -199,7 +210,12 @@
         gram_ref[288:560, :] += second
         return unused
 
-    lax.fori_loop(0, groups * 2, chunk, 0)
+    def pair(index, unused):
+        chunk(index * 2, unused)
+        chunk(index * 2 + 1, unused)
+        return unused
+
+    lax.fori_loop(0, groups, pair, 0)
     cross = gram_ref[288:544, :]
     gram_ref[0:256, :] += cross + cross.T
     total = jnp.sum(acc_ref[3:4, :])
@@ -228,10 +244,12 @@
 
 
 def moment_pass(
-    units_ref, outlier_ref, sum0_ref, sum1_ref, sum2_ref, sum3_ref, tgt_ref, wide_ref, anchors_ref,
+    units_ref, outlier_ref, sum0_ref, sum1_ref, sum2_ref, sum3_ref, tgt_ref, wide_ref, anchors_hbm,
     *refs, total_sources,
 ):
-    *kernel_refs, out_ref, acc_ref, gram_ref, part_ref = refs
+    *kernel_refs, out_ref, acc_ref, gram_ref, part_ref, anchors_ref, arrived = refs
+    copy = pltpu.make_async_copy(anchors_hbm, anchors_ref, arrived)
+    copy.start()
     groups = wide_ref.shape[0]
     outlier = jnp.full((1, UNIT), outlier_ref[0], F32)
     floor = outlier / (1.0 - outlier) * total_sources
@@ -264,6 +282,7 @@
                 acc_ref[:, at] += jnp.dot(weight, value, preferred_element_type=F32)
 
     each_unit(units_ref[0], kernel_refs, block)
+    copy.wait()
     warp_sums(acc_ref, wide_ref, anchors_ref, units_ref[1], out_ref, gram_ref)
 
 
@@ -377,7 +396,7 @@
         out_specs=[WHOLE, WHOLE, SCALAR, SCALAR],
         out_shape=[
             jax.ShapeDtypeStruct((pieces, 80, LANES), BF16),
-            jax.ShapeDtypeStruct((cells + TILE, DEPTH), BF16),
+            jax.ShapeDtypeStruct((cells + UNIT, DEPTH), BF16),
             jax.ShapeDtypeStruct((2,), jnp.int32),
             jax.ShapeDtypeStruct((1,), F32),
         ],
@@ -411,17 +430,19 @@
 
     share = pl.pallas_call(
         functools.partial(moment_pass, total_sources=sources * xs),
-        in_specs=[SCALAR, SCALAR, *[WHOLE] * (xs + 3 + len(KEPT))],
+        in_specs=[SCALAR, SCALAR, *[WHOLE] * (xs + 2), pl.BlockSpec(memory_space=pltpu.HBM), *[WHOLE] * len(KEPT)],
         out_specs=WHOLE,
         out_shape=jax.ShapeDtypeStruct((cs, pieces * 8, LANES), F32),
         scratch_shapes=[
             pltpu.VMEM((8, sources), F32),
             pltpu.VMEM((560, 256), F32),
             pltpu.VMEM((UNIT, GROUP), BF16),
+            pltpu.VMEM((3, 256), F32),
+            pltpu.SemaphoreType.DMA,
         ],
         compiler_params=pltpu.CompilerParams(vmem_limit_bytes=5 << 20),
         name="moment_pass",
-    )(units, outlier, *all_sums, targets, wide, anchors, *kernels)
+    )(units, outlier, *all_sums, targets, wide, pltpu.with_memory_space_constraint(anchors, pltpu.HBM), *kernels)
 
     part = share[0] + lax.ppermute(share[1], "c", [(0, 1), (1, 0)])
     part = part.reshape(pieces, 8, LANES)

time: 136 us -> 131 us (0.963)
  starting transfers between devices: 15.1 us -> 21.7 us
  blocking collectives: 59.3 us -> 53.1 us
  Pallas kernels: 40.7 us -> 37.2 us
    ppermute x1, starting transfers between devices: 0.09 us -> 6.88 us  [local(): part = share[0] + lax.ppermute(share[1], 'c', [(0, 1), (1, 0)])]
    all_to_all x1, blocking collectives: 23 us -> 16.2 us  [local(): part = jnp.sum(lax.all_to_all(part, ('z', 'y'), 0, 0, tiled=True), axis=0)]
    pallas_call x1, Pallas kernels: 19.1 us -> 16.7 us  [local(): pl.pallas_call(kernel_pass, in_specs=[SCALAR, WHOLE, WHOLE, WHOLE], out_s...]
where the time goes in v1:
time: 131 us
  blocking collectives  53.1 us (41%)
  Pallas kernels  37.2 us (28%)
  starting transfers between devices  21.7 us (17%)
  waiting for transfers between devices  15.6 us (12%)
  between operations  2.64 us (2%)
    all_to_all x1, blocking collectives, local(): own = lax.all_to_all(lots, ('z', 'y'), 0, 0, tiled=True)  30.5 us
    pallas_call x1, Pallas kernels, local(): pl.pallas_call(kernel_pass, in_specs=[SCALAR, WHOLE, WHOLE, WHOLE], out_s...  16.7 us
    all_to_all x1, blocking collectives, local(): part = jnp.sum(lax.all_to_all(part, ('z', 'y'), 0, 0, tiled=True), axis=0)  16.2 us
    pallas_call x1, Pallas kernels, local(): pl.pallas_call(functools.partial(moment_pass, total_sources=sources * xs)...  12.3 us
    all_to_all x1, waiting for transfers between devices, spread(): return lax.all_to_all(lots, axes, 0, 0, tiled=True)  8.7 us
    ppermute x6, starting transfers between devices, turned(): lax.ppermute(value, axis, [(i, (i + by) % size) for i in range(size)])  8.5 us
    ppermute x1, starting transfers between devices, local(): part = share[0] + lax.ppermute(share[1], 'c', [(0, 1), (1, 0)])  6.88 us
    all_gather x1, blocking collectives, local(): lax.all_gather(spread(total[None], ('z', 'y')).reshape(pieces * 8, LANES)...  6.3 us
  transfers between devices with their start and end apart: 9, of which 8 were waited for; matrix products, arithmetic and copies ran while one was open for 0% of the time, Pallas kernels for 0%

profile of v1, /device:TPU:1, one launch (start us, length us, event | category | flops | bytes accessed | tf_op | source)
XLA Modules:
  0.0 131.0 jit_solution(13895945494433127723)
XLA Ops:
  1.9 2.7 %prepare.1 = (bf16[32,80,128]{2,1,0:T(8,128)(2,1)S(1)}, bf16[4352,256]{1,0:T(8,128)(2,1)S(1)}, s32[2]{0:T(128)S(1)}, f32[1]{0:T(128)}) custom-call(s32[1]{0:T(128)} %bitcast.core_ref, f32[1]{0:T(128)S(6)} %copy.13.outlier_ref, f32[1]{0:T(128)S(6)} %copy.12.sigma2_ref, s32[8]{0:T(128)} %perm_hbm.1, s32[512]{0:T(512)} %count_hbm.1, bf16[3,4096]{1,0:T(4,128)(2,1)} %xyz_hbm.1, ...), custom_call_target="tpu_custom_call" | custom-call | tf_op jit(solution)/shard_map/prepare/pallas_call | solution.py:393
  4.6 30.5 %all_to_all.15.own_ref = bf16[32,80,128]{2,1,0:T(8,128)(2,1)S(1)} all-to-all(bf16[32,80,128]{2,1,0:T(8,128)(2,1)S(1)} %get-tuple-element.19), channel_id=1, replica_groups=mesh['z'=8,'y'=4,'c'=2,'x'=4] {'z','y'}, dimensions={0} | all-to-all | bytes 1310720 | tf_op jit(solution)/shard_map/all_to_all | solution.py:412
  35.1 2.5 %collective-permute-start = (bf16[32,80,128]{2,1,0:T(8,128)(2,1)S(1)}, bf16[32,80,128]{2,1,0:T(8,128)(2,1)S(1)}, u32[]{:S(2)}, u32[]{:S(2)}) collective-permute-start(bf16[32,80,128]{2,1,0:T(8,128)(2,1)S(1)} %all_to_all.15.own_ref), channel_id=1, source_target_pairs={{0,4},{4,0},{1,5},{5,1},{2,6},{6,2},{3,7},{7,3},{8,12},{12,8},{9,1... | collective-permute-start | bytes 1966088 | tf_op jit(solution)/shard_map/ppermute | solution.py:413
  37.6 1.7 %collective-permute-done.other_ref = bf16[32,80,128]{2,1,0:T(8,128)(2,1)S(1)} collective-permute-done((bf16[32,80,128]{2,1,0:T(8,128)(2,1)S(1)}, bf16[32,80,128]{2,1,0:T(8,128)(2,1)S(1)}, u32[]{:S(2)}, u32[]{:S(2)}) %collective-permute-start) | collective-permute-done | bytes 655392 | tf_op jit(solution)/shard_map/ppermute | solution.py:413
  39.3 16.7 %kernel_pass.1 = (bf16[4,512,2048]{2,1,0:T(8,128)(2,1)S(1)}, bf16[4,512,2048]{2,1,0:T(8,128)(2,1)S(1)}, bf16[4,512,2048]{2,1,0:T(8,128)(2,1)S(1)}, bf16[4,512,20...) custom-call(s32[2]{0:T(128)S(1)} %get-tuple-element.16.units_ref, ...), custom_call_target="tpu_custom_call" | custom-call | tf_op jit(solution)/shard_map/kernel_pass/pallas_call | solution.py:415
  56.1 1.3 collective-permute-start.1
  57.4 2.5 %collective-permute-start.2 = (f32[16,256]{1,0:T(8,128)S(1)}, f32[16,256]{1,0:T(8,128)S(1)}, u32[]{:S(2)}, u32[]{:S(2)}) collective-permute-start(f32[16,256]{1,0:T(8,128)S(1)} %get-tuple-element.20.sum0_ref), channel_id=1, source_target_pairs={{0,2},{1,3},{2,0},{3,1},{4,6},{5,7},{6,4},{7,5},{8,10},{9,11},{10,... | collective-permute-start | bytes 49160 | tf_op jit(solution)/shard_map/ppermute | solution.py:377
  59.8 1.2 collective-permute-start.3
  61.0 0.0 collective-permute-done.1.sum1_ref
  61.0 0.5 collective-permute-done.2.sum2_ref
  61.5 0.9 collective-permute-done.3.sum3_ref
  62.4 0.0 copy-start
  62.4 0.0 copy-start.1
  62.4 12.3 %moment_pass.1 = f32[2,256,128]{2,1,0:T(8,128)S(1)} custom-call(s32[2]{0:T(128)S(1)} %get-tuple-element.16.units_ref, f32[1]{0:T(128)} %get-tuple-element.17.outlier_ref, f32[16,256]{1,0:T(8,128)S(1)} %get-tuple-element.20.sum0_ref, f32[16,256]{1,0:T(8,128)S(1)} %collective-permute-done.1.sum1_ref, f32[16,256]{1,0:T(8,128)S(1)} %collective-permute-done.2.sum2_ref, ...), custom_call_target="tpu_custom_call" | custom-call | tf_op jit(solution)/shard_map/moment_pass/pallas_call | solution.py:431
  74.7 6.9 %collective-permute-start.4 = (f32[256,128]{1,0:T(8,128)S(1)}, f32[256,128]{1,0:T(8,128)S(1)}, u32[]{:S(2)}, u32[]{:S(2)}) collective-permute-start(f32[256,128]{1,0:T(8,128)S(1)} %slice_bitcast_fusion), channel_id=1, source_target_pairs={{0,4},{4,0},{1,5},{5,1},{2,6},{6,2},{3,7},{7,3},{8,12},{12,8},{9,1... | collective-permute-start | bytes 393224 | tf_op jit(solution)/shard_map/ppermute | solution.py:447
  81.6 1.0 collective-permute-done.4
  82.6 16.2 %all_to_all.16 = f32[32,8,128]{2,1,0:T(8,128)S(1)} all-to-all(f32[32,8,128]{2,1,0:T(8,128)S(1)} %fusion.1), channel_id=1, replica_groups=mesh['z'=8,'y'=4,'c'=2,'x'=4] {'z','y'}, dimensions={0} | all-to-all | bytes 262144 | tf_op jit(solution)/shard_map/all_to_all | solution.py:449
  98.9 0.1 collective-permute-start.5
  99.0 3.5 %collective-permute-start.6 = (f32[8,128]{1,0:T(8,128)S(1)}, f32[8,128]{1,0:T(8,128)S(1)}, u32[]{:S(2)}, u32[]{:S(2)}) collective-permute-start(f32[8,128]{1,0:T(8,128)S(1)} %reduce_sum.9.mass_ref), channel_id=1, source_target_pairs={{0,2},{1,3},{2,0},{3,1},{4,6},{5,7},{6,4},{7,5},{8,10},{9,11},{10,... | collective-permute-start | bytes 12296 | tf_op jit(solution)/shard_map/ppermute | solution.py:377
  102.5 0.0 collective-permute-start.7
  102.5 0.1 collective-permute-done.5
  102.7 0.9 collective-permute-done.6
  103.6 1.7 %collective-permute-done.7 = f32[8,128]{1,0:T(8,128)S(1)} collective-permute-done((f32[8,128]{1,0:T(8,128)S(1)}, f32[8,128]{1,0:T(8,128)S(1)}, u32[]{:S(2)}, u32[]{:S(2)}) %collective-permute-start.7) | collective-permute-done | bytes 4128 | tf_op jit(solution)/shard_map/ppermute | solution.py:377
  105.3 0.7 broadcast_in_dim.10
  106.0 3.9 %all-to-all-start.2 = ((f32[32,8,128]{2,1,0:T(8,128)}), f32[32,8,128]{2,1,0:T(8,128)S(1)}, u32[]{:S(2)}, u32[]{:S(2)}) async-start(f32[32,8,128]{2,1,0:T(8,128)} %broadcast_in_dim.10), calls=%async_computation.2 | async-start | bytes 262144 | tf_op jit(solution)/shard_map/all_to_all | solution.py:372
  110.5 8.7 %all-to-all-done.2 = f32[32,8,128]{2,1,0:T(8,128)S(1)} async-done(((f32[32,8,128]{2,1,0:T(8,128)}), f32[32,8,128]{2,1,0:T(8,128)S(1)}, u32[]{:S(2)}, u32[]{:S(2)}) %all-to-all-start.2) | async-done | bytes 131104 | tf_op jit(solution)/shard_map/all_to_all | solution.py:372
  119.2 6.3 %all_gather.3.sums_ref = f32[2,256,128]{2,1,0:T(8,128)S(1)} all-gather(f32[1,256,128]{2,1,0:T(8,128)S(1)} %bitcast.13), channel_id=1, replica_groups=mesh['z'=8,'y'=4,'c'=2,'x'=4] {'c'}, dimensions={0}, use_global_device_ids=true | all-gather | bytes 393216 | tf_op jit(solution)/shard_map/all_gather | solution.py:451
  125.5 0.0 copy-done
  125.5 0.0 copy-done.1
  125.5 5.5 %warp_update.1 = (f32[3,128]{1,0:T(4,128)}, f32[1,128]{1,0:T(1,128)}) custom-call(f32[1]{0:T(128)S(6)} %copy.12.sigma2_ref, f32[1]{0:T(128)S(6)} %copy.14.lambda_ref, f32[3,256]{1,0:T(4,128)S(1)} %copy-done, bf16[3,128]{1,0:T(4,128)(2,1)S(1)} %copy-done.1, f32[8,128]{1,0:T(8,128)S(1)} %reduce_sum.9.mass_ref, f32[2,256,128]{2,1,0:T(8,128)S(1)} %all_gather.3.sums_ref), custom_call_target="tpu_custom_call" | custom-call | tf_op jit(solution)/shard_map/warp_update/pallas_call | solution.py:453
  (4 shorter events, 0.1 us)
Async XLA Ops:
  35.1 4.2 %collective-permute-start = (bf16[32,80,128]{2,1,0:T(8,128)(2,1)S(1)}, bf16[32,80,128]{2,1,0:T(8,128)(2,1)S(1)}, u32[]{:S(2)}, u32[]{:S(2)}) collective-permute-start(bf16[32,80,128]{2,1,0:T(8,128)(2,1)S(1)} %all_to_all.15.own_ref), channel_id=1, source_target_pairs={{0,4},{4,0},{1,5},{5,1},{2,6},{6,2},{3,7},{7,3},{8,12},{12,8},{9,1... | collective-permute-start | bytes 1966088 | tf_op jit(solution)/shard_map/ppermute | solution.py:413
  56.1 4.9 %collective-permute-start.1 = (f32[16,256]{1,0:T(8,128)S(1)}, f32[16,256]{1,0:T(8,128)S(1)}, u32[]{:S(2)}, u32[]{:S(2)}) collective-permute-start(f32[16,256]{1,0:T(8,128)S(1)} %get-tuple-element.20.sum0_ref), channel_id=1, source_target_pairs={{0,1},{1,2},{2,3},{3,0},{4,5},{5,6},{6,7},{7,4},{8,9},{9,10},{10,1... | collective-permute-start | bytes 49160 | tf_op jit(solution)/shard_map/ppermute | solution.py:377
  57.4 4.1 %collective-permute-start.2 = (f32[16,256]{1,0:T(8,128)S(1)}, f32[16,256]{1,0:T(8,128)S(1)}, u32[]{:S(2)}, u32[]{:S(2)}) collective-permute-start(f32[16,256]{1,0:T(8,128)S(1)} %get-tuple-element.20.sum0_ref), channel_id=1, source_target_pairs={{0,2},{1,3},{2,0},{3,1},{4,6},{5,7},{6,4},{7,5},{8,10},{9,11},{10,... | collective-permute-start | bytes 49160 | tf_op jit(solution)/shard_map/ppermute | solution.py:377
  59.8 2.6 %collective-permute-start.3 = (f32[16,256]{1,0:T(8,128)S(1)}, f32[16,256]{1,0:T(8,128)S(1)}, u32[]{:S(2)}, u32[]{:S(2)}) collective-permute-start(f32[16,256]{1,0:T(8,128)S(1)} %get-tuple-element.20.sum0_ref), channel_id=1, source_target_pairs={{0,3},{1,0},{2,1},{3,2},{4,7},{5,4},{6,5},{7,6},{8,11},{9,8},{10,9... | collective-permute-start | bytes 49160 | tf_op jit(solution)/shard_map/ppermute | solution.py:377
  62.4 63.1 %copy-start = (f32[3,256]{1,0:T(4,128)S(1)}, f32[3,256]{1,0:T(4,128)}, u32[]{:S(2)}) copy-start(f32[3,256]{1,0:T(4,128)} %anchors_ref.1) | copy-start | bytes 9220
  62.4 63.1 %copy-start.1 = (bf16[3,128]{1,0:T(4,128)(2,1)S(1)}, bf16[3,128]{1,0:T(4,128)(2,1)}, u32[]{:S(2)}) copy-start(bf16[3,128]{1,0:T(4,128)(2,1)} %xyz_ref.1) | copy-start | bytes 2308
  74.7 7.9 %collective-permute-start.4 = (f32[256,128]{1,0:T(8,128)S(1)}, f32[256,128]{1,0:T(8,128)S(1)}, u32[]{:S(2)}, u32[]{:S(2)}) collective-permute-start(f32[256,128]{1,0:T(8,128)S(1)} %slice_bitcast_fusion), channel_id=1, source_target_pairs={{0,4},{4,0},{1,5},{5,1},{2,6},{6,2},{3,7},{7,3},{8,12},{12,8},{9,1... | collective-permute-start | bytes 393224 | tf_op jit(solution)/shard_map/ppermute | solution.py:447
  98.9 3.7 %collective-permute-start.5 = (f32[8,128]{1,0:T(8,128)S(1)}, f32[8,128]{1,0:T(8,128)S(1)}, u32[]{:S(2)}, u32[]{:S(2)}) collective-permute-start(f32[8,128]{1,0:T(8,128)S(1)} %reduce_sum.9.mass_ref), channel_id=1, source_target_pairs={{0,1},{1,2},{2,3},{3,0},{4,5},{5,6},{6,7},{7,4},{8,9},{9,10},{10,1... | collective-permute-start | bytes 12296 | tf_op jit(solution)/shard_map/ppermute | solution.py:377
  99.0 4.6 %collective-permute-start.6 = (f32[8,128]{1,0:T(8,128)S(1)}, f32[8,128]{1,0:T(8,128)S(1)}, u32[]{:S(2)}, u32[]{:S(2)}) collective-permute-start(f32[8,128]{1,0:T(8,128)S(1)} %reduce_sum.9.mass_ref), channel_id=1, source_target_pairs={{0,2},{1,3},{2,0},{3,1},{4,6},{5,7},{6,4},{7,5},{8,10},{9,11},{10,... | collective-permute-start | bytes 12296 | tf_op jit(solution)/shard_map/ppermute | solution.py:377
  102.5 2.8 %collective-permute-start.7 = (f32[8,128]{1,0:T(8,128)S(1)}, f32[8,128]{1,0:T(8,128)S(1)}, u32[]{:S(2)}, u32[]{:S(2)}) collective-permute-start(f32[8,128]{1,0:T(8,128)S(1)} %reduce_sum.9.mass_ref), channel_id=1, source_target_pairs={{0,3},{1,0},{2,1},{3,2},{4,7},{5,4},{6,5},{7,6},{8,11},{9,8},{10,9... | collective-permute-start | bytes 12296 | tf_op jit(solution)/shard_map/ppermute | solution.py:377
  106.0 13.2 %all-to-all-start.2 = ((f32[32,8,128]{2,1,0:T(8,128)}), f32[32,8,128]{2,1,0:T(8,128)S(1)}, u32[]{:S(2)}, u32[]{:S(2)}) async-start(f32[32,8,128]{2,1,0:T(8,128)} %broadcast_in_dim.10), calls=%async_computation.2 | async-start | bytes 262144 | tf_op jit(solution)/shard_map/all_to_all | solution.py:372
